TPU v7x, 256 devices: a whole 4x4x8 slice. The times are simulated.
256 devices in a mesh: win: 4 (over y), space: 64 (over z, x, core).
Axes of the slice: x: 4, y: 4, z: 8, core: 2. Of those that a mesh axis runs over, the one named last changes fastest.
Arguments:
- multipliers: float32 [8, 12, 512, 256], P('win', None, 'space'), may hold values from -6 to 6
- increments: float32 [8, 12, 512, 256], P('win', None, 'space'), may hold values from -6 to 6
- background: float32 [8, 12, 512, 256], P('win', None, 'space'), may hold values from -1.8 to 2, as said below
- error_variance: float32 [8, 12, 512, 256], P('win', None, 'space'), may hold values from 0.25 to 4
- report_weights: float32 [8, 4, 16384], P('win', None, 'space'), may hold values from -6 to 6
- report_variance: float32 [8, 4, 16384], P('win', None, 'space'), may hold values from 0.25 to 4
- report_cells: int32 [8, 4, 16384], P('win', None, 'space'), may hold values from 0 to 24319, as said below
- report_offsets: float32 [8, 4, 2, 16384], P('win', None, None, 'space'), may hold values from 0 to 1
- report_counts: int32 [8, 4, 4096], P('win', None, 'space'), may hold values from 1 to 4, as said below
Outputs:
- model_residual: float32 [8, 12, 512, 256], P('win', None, 'space')
- report_residual: float32 [8, 4, 16384], P('win', None, 'space')
- adjoint_image: float32 [8, 12, 512, 256], P('win', None, 'space')
Inputs may be any that keep to these rules, and one draw needn't show every extreme that they name: `report_cells`: entry p of slot s encodes channel c, strip row r below 7 and column q as p = c * 8 * 256 + r * 256 + q, the rows counted inside the slot's home strip. `report_counts`: entry m * 64 + o counts the live slots from home strip m to owner o at that step; they are the first ones of their 4. `background`: channels 3 l and 3 l + 1 hold velocities between -1.8 and 1.8; channel 3 l + 2 holds depths between 0.3 and 2.
All inputs are finite; a program needn't handle non-finite values.
Results may differ from a plain program's by a relative error of at most 0.0003.
Values sent between devices are 32-bit elements; how exact they have to be, the bound alone decides.
No kernel may reach another device: no remote copies, remote signals or barrier semaphores. Data moves between devices by JAX's collectives and lax.ppermute only.
A program may use at most 64 MiB of HBM per device.

v0:
```python
import jax
import jax.numpy as jnp
import numpy as np
from jax import lax
from jax.experimental import pallas as pl
from jax.experimental.pallas import tpu as pltpu
from jax.sharding import PartitionSpec as P

coupling = np.array(
    [[1.0, 0.55, 0.3, 0.15], [0.5, 0.9, 0.45, 0.25], [0.3, 0.4, 0.8, 0.35], [0.1, 0.2, 0.35, 0.7]],
    np.float32,
)
LEVELS = 4
VARS = 3
STEPS = 4
STRIP = 8
HALO = 4
EXT = STRIP + 2 * HALO
NX = 256
OWNERS = 64
CAP = 4
PARTS = 8
FIELD_TILES = VARS * HALO
NEAR = FIELD_TILES + VARS * (HALO - 1)
OUTER = FIELD_TILES
REPORTS = OUTER + 2
FAR = REPORTS + 3
CODES = VARS * STRIP * LEVELS
TILES = CODES // 8
FIRST_FIELD = [VARS * sum(STRIP + 2 * i for i in range(j)) for j in range(STEPS + 1)]
FIELDS_COST = 2
OUTER_COST = 0.01
ADJOINT_COST = 30
SCALE = 0.05
f32 = jnp.float32
bf16 = jnp.bfloat16
params = pltpu.CompilerParams(vmem_limit_bytes=20 * 2**20)


def east(z):
    return pltpu.roll(z, NX - 1, 1)


def west(z):
    return pltpu.roll(z, 1, 1)


def mix_weights(matrix):
    level = lax.broadcasted_iota(jnp.int32, (PARTS, NX), 0) % LEVELS
    weights = []
    for shift in range(1 - LEVELS, LEVELS):
        weight = jnp.zeros((PARTS, NX), f32)
        for l in range(LEVELS):
            if 0 <= l + shift < LEVELS:
                weight = jnp.where(level == l, float(matrix[l, l + shift]), weight)
        weights.append((shift, weight))
    return weights


def mix(z, weights):
    total = None
    for shift, weight in weights:
        term = weight * (z if shift == 0 else pltpu.roll(z, (-shift) % PARTS, 0))
        total = term if total is None else total + term
    return total


def split(x):
    high = x.astype(bf16)
    return high, (x - high.astype(f32)).astype(bf16)


def parity():
    return lax.axis_index("space") % 2 == 0


def state_rows(block):
    return jnp.swapaxes(block, 0, 1)


def owner_of_lane():
    lane = lax.broadcasted_iota(jnp.int32, (OWNERS, NX), 1)
    return lane // CAP == lax.broadcasted_iota(jnp.int32, (OWNERS, NX), 0)


def decode(report):
    p = report.astype(jnp.int32)
    channel = p >> 11
    level = (channel * 11) >> 5
    variable = channel - 3 * level
    code = (variable * STRIP + ((p >> 8) & 7)) * LEVELS + level
    return jnp.where(p < 0, -1024, code), p & (NX - 1)


def column_weights(report, n):
    _, column = decode(report[0, n : n + 1])
    share = report[1, n : n + 1]
    place = lax.broadcasted_iota(jnp.int32, (NX, NX), 0)
    following = jnp.where(place == ((column + 1) & (NX - 1)), share, 0.0)
    return split(jnp.where(place == column, 1.0 - share, following))


def one_hot_columns(column):
    place = lax.broadcasted_iota(jnp.int32, (NX, NX), 0)
    return jnp.where(place == column, 1.0, 0.0).astype(f32).astype(bf16)


def lower_half():
    return lax.broadcasted_iota(jnp.int32, (PARTS, NX), 0) < LEVELS


def code_tiles(rows):
    return [v * STRIP // 2 + t for v in range(VARS) for t in range(rows[0] // 2, rows[-1] // 2 + 1)]


def window_tiles(pair):
    first = lower_half()
    one = jnp.where(first, pair[0], pltpu.roll(pair[1], LEVELS, 0))
    two = jnp.where(first, pltpu.roll(pair[0], LEVELS, 0), pair[1])
    return one, two


def chosen_rows(low_end, rows, first, last):
    return jnp.where(low_end, rows[first:last], rows[STRIP - last : STRIP - first])


def near_halo(low_end, inc_rows, bg_rows, out):
    for v in range(VARS):
        at = v * HALO
        out[at : at + HALO] = chosen_rows(low_end, inc_rows[v], 0, HALO)
        at = FIELD_TILES + v * (HALO - 1)
        out[at : at + HALO - 1] = chosen_rows(low_end, bg_rows[v], 0, HALO - 1)


def far_halo(low_end, mult_rows, bg_rows, rep, out):
    for v in range(VARS):
        at = v * HALO
        out[at : at + HALO] = chosen_rows(low_end, mult_rows[v], 0, HALO)
        if v > 0:
            at = OUTER + v - 1
            out[at : at + 1] = chosen_rows(low_end, bg_rows[v], HALO - 1, HALO)
    out[REPORTS:] = rep[...]


def pack_kernel(
    inc, bg, mult, cells, offsets, counts,
    near, inner, rep, inc_rows, bg_rows, mult_rows,
    raw, raw_cells, raw_offsets, raw_counts, sems,
):
    copies = []
    for n, (source, target) in enumerate(
        (
            (inc, raw.at[0]),
            (bg, raw.at[1]),
            (mult, raw.at[2]),
            (cells, raw_cells),
            (offsets, raw_offsets),
            (counts, raw_counts),
        )
    ):
        copies.append(pltpu.make_async_copy(source, target, sems.at[n]))
        copies[n].start()
    even = parity()
    odd = jnp.logical_not(even)
    for f, rows_out in enumerate((inc_rows, bg_rows, mult_rows)):
        copies[f].wait()
        for v in range(VARS):
            rows_out[v] = state_rows(raw[f, :, v])
    near_halo(even, inc_rows, bg_rows, near)
    near_halo(odd, inc_rows, bg_rows, inner)
    for copy in copies[3:]:
        copy.wait()
    slot = lax.broadcasted_iota(jnp.int32, (PARTS, NX), 1) % CAP
    count = jnp.concatenate([raw_counts[0], raw_counts[1]], axis=0).astype(f32).astype(bf16)
    spread = jnp.where(owner_of_lane(), 1.0, 0.0).astype(f32).astype(bf16)
    live = slot.astype(f32) < jnp.dot(count, spread, preferred_element_type=f32)
    cell = jnp.concatenate([raw_cells[0], raw_cells[1]], axis=0).astype(f32)
    rep[0] = jnp.where(live, cell, -1.0)
    for k in range(2):
        for j in range(STEPS):
            for side in range(2):
                rep[1 + side, pl.ds(k * STEPS + j, 1), :] = raw_offsets[k, j, pl.ds(side, 1), :]
    far_halo(odd, mult_rows, bg_rows, rep, inner.at[NEAR:])


def sample(rows, j, rep, weights, rests, vals):
    pairs = [
        window_tiles((rows[v][r], rows[v][r + 1])) for v in range(VARS) for r in range(0, STRIP, 2)
    ]
    place = lax.broadcasted_iota(jnp.int32, (PARTS, NX), 0)
    for k in range(2):
        n = k * STEPS + j
        high, low = split(jnp.concatenate([pair[k] for pair in pairs], axis=0))
        code, _ = decode(rep[0, n : n + 1])
        picked = jnp.dot(
            jnp.concatenate([high, low], axis=0), weights[n], preferred_element_type=f32
        )
        rest = jnp.dot(high, rests[n], preferred_element_type=f32)
        sums = [jnp.zeros((PARTS, NX), f32) for _ in range(2)]
        for t in range(TILES):
            at = t * 8
            value = picked[at : at + 8] + (picked[CODES + at : CODES + at + 8] + rest[at : at + 8])
            sums = [
                jnp.where(code == place + at, value, sums[0]),
                jnp.where(code == place + (at - LEVELS), value, sums[1]),
            ]
        b = rep[2, n : n + 1]
        value = (1.0 - b) * sums[0] + b * sums[1]
        vals[pl.ds(n, 1), :] = jnp.sum(value, axis=0, keepdims=True)


def tangent_rows(get, back, raised, weights, rows, put):
    for row in sorted({near for row in rows for near in (row - 1, row, row + 1)}):
        raised[row] = mix(get(2, row), weights)
    for row in rows:
        ub, vb, hb = back(0, row), back(1, row), back(2, row)
        centre = [get(v, row) for v in range(VARS)]
        up = [get(v, row + 1) for v in range(VARS)]
        down = [get(v, row - 1) for v in range(VARS)]
        e = [east(z) for z in centre]
        w = [west(z) for z in centre]
        cols = [e[v] - w[v] for v in range(VARS)]
        slopes = [up[v] - down[v] for v in range(VARS)]
        smooth = [up[v] + down[v] + (e[v] + w[v]) for v in range(VARS)]
        lift = raised[row]
        push_c = east(lift) - west(lift)
        push_r = raised[row + 1] - raised[row - 1]
        new = [
            0.98 * centre[0]
            + 0.03 * centre[1]
            + 0.005 * smooth[0]
            - push_c
            - (ub * cols[0] + vb * slopes[0]),
            0.98 * centre[1]
            - 0.03 * centre[0]
            + 0.005 * smooth[1]
            - push_r
            - (ub * cols[1] + vb * slopes[1]),
            0.98 * centre[2]
            + 0.005 * smooth[2]
            - hb * (cols[0] + slopes[1])
            - (ub * cols[2] + vb * slopes[2]),
        ]
        for v in range(VARS):
            put(v, row, new[v])


def inside(step):
    return range(HALO + 1 + step, HALO + STRIP - 1 - step)


def prepare_kernel(
    inc_rows, bg_rows, mult_rows, rep, far, along, rests, vals, known, raised
):
    far_halo(parity(), mult_rows, bg_rows, rep, far)
    for n in range(2 * STEPS):
        along[n], rests[n] = column_weights(rep, n)
    vals[...] = jnp.zeros((PARTS, NX), f32)
    rows = [[inc_rows[v, r] for r in range(STRIP)] for v in range(VARS)]
    sample(rows, 0, rep, along, rests, vals)
    weights = mix_weights(SCALE * coupling)
    for step in range(STEPS - 1):
        before = inc_rows if step == 0 else known.at[step - 1]

        def put(v, row, value):
            known[step, v, row - HALO] = value

        tangent_rows(
            lambda v, row: before[v, row - HALO],
            lambda v, row: SCALE * bg_rows[v, row - HALO],
            raised,
            weights,
            inside(step),
            put,
        )


def edges():
    s = lax.axis_index("space")
    top = jnp.where(s > 0, 1.0, 0.0).astype(f32)
    bottom = jnp.where(s < OWNERS - 1, 1.0, 0.0).astype(f32)
    return top, bottom


def both_sides(even, a, b):
    return jnp.where(even, b, a), jnp.where(even, a, b)


def send_out(vals, owned, owned_variance, expected, send, packed, sem):
    own = jnp.concatenate([owned[0], owned[1]], axis=0)
    expected[...] = own * jnp.concatenate([owned_variance[0], owned_variance[1]], axis=0)
    slot = lax.broadcasted_iota(jnp.int32, (PARTS, NX), 1) % CAP
    pieces = []
    for piece in (pltpu.roll(own, CAP, 1), own, pltpu.roll(own, NX - CAP, 1), vals[...]):
        for i in range(CAP):
            pieces.append(jnp.where(slot == i, piece, 0.0))
    chosen = jnp.where(owner_of_lane(), 1.0, 0.0).astype(f32).astype(bf16)
    both = lax.dot_general(
        chosen,
        jnp.concatenate(split(jnp.concatenate(pieces, axis=0)), axis=0),
        (((1,), (1,)), ((), ())),
        preferred_element_type=f32,
    )
    lanes = 4 * CAP * PARTS
    packed[...] = both[:, :lanes] + both[:, lanes:]
    copy = pltpu.make_async_copy(packed, send, sem)
    copy.start()
    return copy


def tangent_kernel(
    inc_rows, bg_rows, rep, along, rests, early, known, got_a, got_near, owned, owned_variance,
    final0, final1, send, expected, back,
    state, raised, vals, packed, sem,
):
    even = parity()
    top, bottom = edges()
    end = HALO + STRIP
    for v in range(VARS):
        at = v * HALO
        low, high = both_sides(even, got_a[at : at + HALO], got_near[at : at + HALO])
        state[0, v, :HALO] = low
        state[0, v, end:] = high
        at = FIELD_TILES + v * (HALO - 1)
        low, high = both_sides(even, got_a[at : at + HALO - 1], got_near[at : at + HALO - 1])
        back[v, 1:HALO] = SCALE * low
        back[v, HALO:end] = SCALE * bg_rows[v]
        back[v, end : EXT - 1] = SCALE * high
        back[v, 0] = jnp.zeros((PARTS, NX), f32)
        back[v, EXT - 1] = jnp.zeros((PARTS, NX), f32)

    weights = mix_weights(SCALE * coupling)
    vals[...] = early[...]

    def get_at(j, v, row):
        if j == 0 and HALO <= row < end:
            return inc_rows[v, row - HALO]
        if j > 0 and row in inside(j - 1):
            return known[j - 1, v, row - HALO]
        return state[j, v, row]

    def advance(j, rows):
        def put(v, row, value):
            if row < HALO:
                value = value * top
            elif row >= end:
                value = value * bottom
            state[j + 1, v, row] = value

        tangent_rows(
            lambda v, row: get_at(j, v, row), lambda v, row: back[v, row], raised, weights, rows, put
        )

    for j in range(STEPS - 1):
        advance(j, [row for row in range(j + 2, EXT - 2 - j) if row not in inside(j)])
        rows = [[get_at(j + 1, v, HALO + r) for r in range(STRIP)] for v in range(VARS)]
        sample(rows, j + 1, rep, along, rests, vals)
    copy = send_out(vals, owned, owned_variance, expected, send, packed, sem)
    @pl.when(lax.axis_index("space") >= 0)
    def while_it_leaves():
        for j in range(STEPS - 1):
            advance(j, [j + 1, EXT - 2 - j])
        advance(STEPS - 1, list(range(HALO, end)))
        last = STEPS
        for v in range(VARS):
            value = state_rows(state[last, v, HALO : HALO + STRIP])
            final0[:, v] = value[:LEVELS]
            final1[:, v] = value[LEVELS:]

    copy.wait()


def outer_kernel(mult_rows, inner, far, final1, out, final_out, mine, outermost, sides):
    even = parity()
    half = EXT // 2
    final_out[...] = final1[...]
    for v in range(VARS):
        at = v * HALO
        low, high = both_sides(
            even, inner[NEAR + at : NEAR + at + HALO], far[at : at + HALO]
        )
        rows = (
            [low[i] for i in range(HALO)]
            + [mult_rows[v, r] for r in range(STRIP)]
            + [high[i] for i in range(HALO)]
        )
        for i in range(half):
            n = v * half + i
            out[n], mine[n] = window_tiles((rows[i], rows[i + half]))
    for v in (1, 2):
        at = OUTER + v - 1
        low, high = both_sides(even, inner[NEAR + at], far[at])
        outermost[v - 1, 0], outermost[v - 1, 1] = SCALE * low, SCALE * high
    for n in range(3):
        at = REPORTS + n
        sides[0, n], sides[1, n] = both_sides(even, inner[NEAR + at], far[at])


def adjoint_step(step, now, later, back, flux, weights, added):
    top, bottom = edges()
    for row in range(step, EXT - step):
        vb, hb = back(1, row), back(2, row)
        au, av, ah = now[0, row], now[1, row], now[2, row]
        flux[0, row] = vb * au
        flux[1, row] = hb * ah + vb * av
        flux[2, row] = vb * ah
    for row in range(step + 1, EXT - 1 - step):
        ub, hb = back(0, row), back(2, row)
        centre = [now[v, row] for v in range(VARS)]
        au, av, ah = centre
        across = [hb * ah + ub * au, ub * av, ub * ah]
        lift = mix((east(au) - west(au)) + (now[1, row + 1] - now[1, row - 1]), weights)
        turn = [0.98 * au - 0.03 * av, 0.98 * av + 0.03 * au, 0.98 * ah + lift]
        for v in range(VARS):
            spread = 0.005 * centre[v]
            value = (
                turn[v]
                + (east(spread + across[v]) + west(spread - across[v]))
                + (0.005 * (now[v, row + 1] + now[v, row - 1]) + (flux[v, row + 1] - flux[v, row - 1]))
            )
            value = value + added(v, row)
            if row < HALO:
                value = value * top
            elif row >= HALO + STRIP:
                value = value * bottom
            later[v, row] = value


def fields_kernel(
    mult, variance, inc, got, expected, rep, sides, final0,
    report_out, fields, mult_out, model_out,
    raw, sems,
):
    copies = []
    for n, (source, target) in enumerate(
        ((mult, mult_out), (variance, raw.at[0]), (inc, raw.at[1]))
    ):
        copies.append(pltpu.make_async_copy(source, target, sems.at[n]))
        copies[n].start()
    chosen = jnp.where(owner_of_lane(), 1.0, 0.0).astype(f32).astype(bf16)
    spread = jnp.dot(
        jnp.concatenate(split(jnp.transpose(got[...])), axis=0),
        chosen,
        preferred_element_type=f32,
    )
    lanes = 4 * CAP * PARTS
    spread = spread[:lanes] + spread[lanes:]
    slot = lax.broadcasted_iota(jnp.int32, (PARTS, NX), 1) % CAP
    loads = []
    for g in range(4):
        value = jnp.zeros((PARTS, NX), f32)
        for i in range(CAP):
            at = (g * CAP + i) * PARTS
            value = jnp.where(slot == i, spread[at : at + PARTS], value)
        loads.append(value)
    for k in range(2):
        at = k * STEPS
        report_out[k] = expected[pl.ds(at, STEPS), :] + loads[3][at : at + STEPS]
    place = lax.broadcasted_iota(jnp.int32, (PARTS, NX), 0)
    first = lower_half()
    transposed = (((1,), (1,)), ((), ()))

    def field(report, load, j, rows):
        tiles = code_tiles(rows)
        count = 8 * len(tiles)
        windows = []
        for k in range(2):
            n = k * STEPS + j
            code, column = decode(report[0, n : n + 1])
            a, b = report[1, n : n + 1], report[2, n : n + 1]
            weight = load[n : n + 1]
            parts = []
            for share in ((1.0 - a) * weight, a * weight):
                own, following = (1.0 - b) * share, b * share
                block = []
                for t in tiles:
                    tile = jnp.where(code == place + (8 * t - LEVELS), following, 0.0)
                    block.append(jnp.where(code == place + 8 * t, own, tile))
                parts += list(split(jnp.concatenate(block, axis=0)))
            out = lax.dot_general(
                jnp.concatenate(parts, axis=0),
                one_hot_columns(column),
                transposed,
                preferred_element_type=f32,
            )
            total = out[:count] + out[count : 2 * count]
            total = total + west(out[2 * count : 3 * count] + out[3 * count :])
            windows.append(total)
        for at, t in enumerate(tiles):
            one, two = (w[8 * at : 8 * at + 8] for w in windows)
            v, r = t // (STRIP // 2), 2 * (t % (STRIP // 2))
            yield v, r, jnp.where(first, one, pltpu.roll(two, LEVELS, 0))
            yield v, r + 1, jnp.where(first, pltpu.roll(one, LEVELS, 0), two)

    for j in range(STEPS):
        base = FIRST_FIELD[j]
        for v, r, tile in field(rep, loads[1], j, list(range(STRIP))):
            fields[base + v * (STRIP + 2 * j) + j + r] = tile
        if j > 0:
            for v, r, tile in field(sides.at[0], loads[0], j, list(range(STRIP - j, STRIP))):
                if r >= STRIP - j:
                    fields[base + v * (STRIP + 2 * j) + j + r - STRIP] = tile
            for v, r, tile in field(sides.at[1], loads[2], j, list(range(j))):
                if r < j:
                    fields[base + v * (STRIP + 2 * j) + j + r + STRIP] = tile
    for copy in copies:
        copy.wait()
    for c in range(PARTS):
        model = raw[0, c] * mult_out[c] + raw[1, c]
        model_out[c] = model if c < LEVELS else model - final0[c - LEVELS]


def adjoint_kernel(
    mult, outer, mine, outermost, back, fields,
    image,
    state, flux,
):
    def backdrop(v, row):
        if v > 0 and row in (0, EXT - 1):
            return outermost[v - 1, 1 if row else 0]
        return back[v, row]

    first = lower_half()
    half = EXT // 2
    for v in range(VARS):
        for i in range(half):
            own, after = mine[v * half + i], outer[v * half + i]
            state[0, v, i] = -jnp.where(first, own, pltpu.roll(after, LEVELS, 0))
            state[0, v, i + half] = -jnp.where(first, pltpu.roll(own, LEVELS, 0), after)
    weights = mix_weights(SCALE * coupling.T)
    for step, j in enumerate(reversed(range(STEPS))):
        now, later = state.at[step % 2], state.at[(step + 1) % 2]

        def added(v, row):
            return fields[FIRST_FIELD[j] + v * (STRIP + 2 * j) + row - step - 1]

        adjoint_step(step, now, later, backdrop, flux, weights, added)
    last = STEPS % 2
    for v in range(VARS):
        image[:, v] = mult[:, v] + state_rows(state[last, v, HALO : HALO + STRIP])


def finish_kernel(
    image, report, model, incoming, image_out, report_out, model_out, first, sems
):
    copies = [
        pltpu.make_async_copy(image, image_out, sems.at[0]),
        pltpu.make_async_copy(model.at[LEVELS:], model_out.at[LEVELS:], sems.at[1]),
        pltpu.make_async_copy(report, report_out, sems.at[2]),
        pltpu.make_async_copy(first, model_out.at[:LEVELS], sems.at[3]),
    ]
    for copy in copies[:3]:
        copy.start()
    first[...] = model[:LEVELS] - incoming[...]
    copies[3].start()
    for copy in copies:
        copy.wait()


def vmem(count):
    return [pl.BlockSpec(memory_space=pltpu.VMEM)] * count


def hbm(count):
    return [pl.BlockSpec(memory_space=pltpu.HBM)] * count


def far_from_core(x):
    return pltpu.with_memory_space_constraint(x, pltpu.HBM)


def shaped(*shape, kind=f32):
    return jax.ShapeDtypeStruct(shape, kind)


def cost(kernel_us):
    return pl.CostEstimate(flops=int(kernel_us * 1e9), bytes_accessed=int(kernel_us * 3e6), transcendentals=0)


def per_device(
    multipliers,
    increments,
    background,
    error_variance,
    report_weights,
    report_variance,
    report_cells,
    report_offsets,
    report_counts,
):
    mult, inc, bg, variance = (
        x.reshape(PARTS, VARS, STRIP, NX)
        for x in (multipliers, increments, background, error_variance)
    )
    count = lax.axis_size("space")
    wins = lax.axis_size("win")
    tile = (PARTS, NX)
    rows = shaped(VARS, STRIP, *tile)
    extended = shaped(VARS, EXT, *tile)
    whole = shaped(PARTS, VARS, STRIP, NX)
    scratch = pltpu.VMEM(whole.shape, f32)
    near, inner, rep, inc_rows, bg_rows, mult_rows = pl.pallas_call(
        pack_kernel,
        name="pack",
        out_shape=(
            shaped(NEAR, *tile),
            shaped(NEAR + FAR, *tile),
            shaped(3, *tile),
            rows,
            rows,
            rows,
        ),
        in_specs=hbm(6),
        out_specs=vmem(6),
        scratch_shapes=[
            pltpu.VMEM((3, *whole.shape), f32),
            pltpu.VMEM(report_cells.shape, jnp.int32),
            pltpu.VMEM(report_offsets.shape, f32),
            pltpu.VMEM(report_counts.shape, jnp.int32),
            pltpu.SemaphoreType.DMA((6,)),
        ],
        compiler_params=params,
    )(
        *(
            far_from_core(x)
            for x in (inc, bg, mult, report_cells, report_offsets, report_counts)
        )
    )
    both = lambda pairs: pairs + [(target, source) for source, target in pairs]
    near = lax.ppermute(near, "space", both([(i, i + 1) for i in range(1, count - 1, 2)]))
    inner = lax.ppermute(inner, "space", both([(i, i + 1) for i in range(0, count, 2)]))
    hot = shaped(2 * STEPS, NX, NX, kind=bf16)
    far, along, rests, early, known = pl.pallas_call(
        prepare_kernel,
        name="prepare",
        out_shape=(
            shaped(FAR, *tile), hot, hot, shaped(*tile), shaped(STEPS - 1, VARS, STRIP, *tile)
        ),
        in_specs=vmem(4),
        out_specs=vmem(5),
        scratch_shapes=[pltpu.VMEM((EXT, *tile), f32)],
        cost_estimate=cost(2),
        compiler_params=params,
    )(inc_rows, bg_rows, mult_rows, rep)
    far = lax.ppermute(far, "space", both([(i, i + 1) for i in range(1, count - 1, 2)]))
    final0, final1, send, expected, back = pl.pallas_call(
        tangent_kernel,
        name="tangent",
        out_shape=(
            shaped(LEVELS, VARS, STRIP, NX),
            shaped(LEVELS, VARS, STRIP, NX),
            shaped(OWNERS, 4 * CAP * PARTS),
            shaped(*tile),
            extended,
        ),
        in_specs=vmem(11),
        out_specs=vmem(2) + hbm(1) + vmem(2),
        scratch_shapes=[
            pltpu.VMEM((STEPS + 1, *extended.shape), f32),
            pltpu.VMEM((EXT, *tile), f32),
            pltpu.VMEM(tile, f32),
            pltpu.VMEM((OWNERS, 4 * CAP * PARTS), f32),
            pltpu.SemaphoreType.DMA,
        ],
        cost_estimate=cost(2),
        compiler_params=params,
    )(
        inc_rows, bg_rows, rep, along, rests, early, known, inner, near, report_weights,
        report_variance,
    )
    got = lax.all_to_all(send, "space", split_axis=0, concat_axis=0, tiled=True)
    folded = shaped(VARS * EXT // 2, *tile)
    half = shaped(LEVELS, VARS, STRIP, NX)
    outer, final1, mine, outermost, sides = pl.pallas_call(
        outer_kernel,
        name="outer",
        out_shape=(
            folded, half, folded, shaped(2, 2, *tile), shaped(2, 3, *tile)
        ),
        in_specs=vmem(4),
        out_specs=vmem(5),
        cost_estimate=cost(OUTER_COST),
        compiler_params=params,
    )(mult_rows, inner, far, final1)
    incoming = lax.ppermute(final1, "win", [(i, i + 1) for i in range(wins - 1)])
    outer = lax.ppermute(outer, "win", [(i + 1, i) for i in range(wins - 1)])
    report, fields, mult_near, model = pl.pallas_call(
        fields_kernel,
        name="fields",
        out_shape=(
            shaped(2, STEPS, NX), shaped(FIRST_FIELD[STEPS], *tile), whole, whole
        ),
        in_specs=hbm(3) + vmem(5),
        out_specs=vmem(4),
        scratch_shapes=[pltpu.VMEM((2, *whole.shape), f32), pltpu.SemaphoreType.DMA((3,))],
        cost_estimate=cost(FIELDS_COST),
        compiler_params=params,
    )(
        *(far_from_core(x) for x in (mult, variance, inc)),
        got, expected, rep, sides, final0,
    )
    image = pl.pallas_call(
        adjoint_kernel,
        name="adjoint",
        out_shape=whole,
        in_specs=vmem(6),
        out_specs=vmem(1)[0],
        scratch_shapes=[
            pltpu.VMEM((2, *extended.shape), f32),
            pltpu.VMEM(extended.shape, f32),
        ],
        cost_estimate=cost(ADJOINT_COST),
        compiler_params=params,
    )(mult_near, outer, mine, outermost, back, fields)
    image, report, model = pl.pallas_call(
        finish_kernel,
        name="finish",
        out_shape=(whole, shaped(2, STEPS, NX), whole),
        in_specs=vmem(4),
        out_specs=hbm(3),
        scratch_shapes=[pltpu.VMEM(half.shape, f32), pltpu.SemaphoreType.DMA((4,))],
        compiler_params=params,
    )(image, report, model, incoming)
    return model.reshape(multipliers.shape), report, image.reshape(multipliers.shape)


def solution(mesh):
    state = P("win", None, "space", None)
    slots = P("win", None, "space")
    return jax.shard_map(
        per_device,
        mesh=mesh,
        in_specs=(state, state, state, state, slots, slots, slots, P("win", None, None, "space"), slots),
        out_specs=(state, slots, state),
        check_vma=False,
    )
```

profile of v0, /device:TPU:1, one launch (start us, length us, event | category | flops | bytes accessed | tf_op | source)
XLA Modules:
  0.0 38.9 jit_solution(17217740666028376793)
XLA Ops:
  0.6 1.4 %pack.1 = (f32[21,8,256]{2,1,0:T(8,128)S(1)}, f32[38,8,256]{2,1,0:T(8,128)S(1)}, f32[3,8,256]{2,1,0:T(8,128)S(1)}, f32[3,8,8,256]{3,2,1,0:T(8,128)S(1)}, f32[3,8...) custom-call(f32[8,3,8,256]{3,2,1,0:T(8,128)} %bitcast.14, f32[8,3,8,256]{3,2,1,0:T(8,128)} %bitcast.11, ...), custom_call_target="tpu_custom_call" | custom-call | tf_op jit(solution)/shard_map/pack/pallas_call | solution.py:602
  2.0 3.3 %collective-permute-start = (f32[38,8,256]{2,1,0:T(8,128)S(1)}, f32[38,8,256]{2,1,0:T(8,128)S(1)}, u32[]{:S(2)}, u32[]{:S(2)}) collective-permute-start(f32[38,8,256]{2,1,0:T(8,128)S(1)} %get-tuple-element.39), channel_id=1, source_target_pairs={{0,1},{2,3},{4,5},{6,7},{8,9},{10,11},{12,13},{14,15},{16,17},{18,... | collective-permute-start | bytes 933896 | tf_op jit(solution)/shard_map/ppermute | solution.py:631
  5.3 1.9 %collective-permute-start.1 = (f32[21,8,256]{2,1,0:T(8,128)S(1)}, f32[21,8,256]{2,1,0:T(8,128)S(1)}, u32[]{:S(2)}, u32[]{:S(2)}) collective-permute-start(f32[21,8,256]{2,1,0:T(8,128)S(1)} %get-tuple-element.40), channel_id=1, source_target_pairs={{1,2},{3,4},{5,6},{7,8},{9,10},{11,12},{13,14},{15,16},{17,18},{19... | collective-permute-start | bytes 516104 | tf_op jit(solution)/shard_map/ppermute | solution.py:630
  7.3 0.0 copy-start
  7.3 0.0 copy-start.1
  7.3 1.1 %prepare.1 = (f32[17,8,256]{2,1,0:T(8,128)S(1)}, bf16[8,256,256]{2,1,0:T(8,128)(2,1)S(1)}, bf16[8,256,256]{2,1,0:T(8,128)(2,1)S(1)}, f32[8,256]{1,0:T(8,128)S(1)}, f32[3,3,8,8,256]{4,3,2,1,0:T(8,128)S(1)}) custom-call(f32[3,8,8,256]{3,2,1,0:T(8,128)S(1)} %get-tuple-element.31.inc_rows, f32[3,8,8,256]{3,2,1,0:T(8,128)S(1)} %get-tuple-element.32.bg_rows, ...), custom_call_target="tpu_custom_call" | custom-call | flops 2000000000 | bytes 6000000 | tf_op jit(solution)/shard_map/prepare/pallas_call | solution.py:633
  8.4 3.6 %collective-permute-start.2 = (f32[17,8,256]{2,1,0:T(8,128)S(1)}, f32[17,8,256]{2,1,0:T(8,128)S(1)}, u32[]{:S(2)}, u32[]{:S(2)}) collective-permute-start(f32[17,8,256]{2,1,0:T(8,128)S(1)} %get-tuple-element.43), channel_id=1, source_target_pairs={{1,2},{3,4},{5,6},{7,8},{9,10},{11,12},{13,14},{15,16},{17,18},{19... | collective-permute-start | bytes 417800 | tf_op jit(solution)/shard_map/ppermute | solution.py:645
  12.0 0.0 collective-permute-done.1.got_near
  12.1 0.0 collective-permute-done.got_a.inner
  12.1 0.0 copy-done
  12.1 0.0 copy-done.1
  12.1 1.8 %tangent.1 = (f32[4,3,8,256]{3,2,1,0:T(8,128)S(1)}, f32[4,3,8,256]{3,2,1,0:T(8,128)S(1)}, f32[64,128]{1,0:T(8,128)}, f32[8,256]{1,0:T(8,128)S(1)}, f32[3,16,8,256]{3,2,1,0:T(8,128)S(1)}) custom-call(f32[3,8,8,256]{3,2,1,0:T(8,128)S(1)} %get-tuple-element.31.inc_rows, f32[3,8,8,256]{3,2,1,0:T(8,128)S(1)} %get-tuple-element.32.bg_rows, ...), custom_call_target="tpu_custom_call" | custom-call | flops 2000000000 | bytes 6000000 | tf_op jit(solution)/shard_map/tangent/pallas_call | solution.py:646
  13.9 11.7 %all-to-all-start = ((f32[64,1,128]{2,1,0:T(1,128)}), f32[64,1,128]{2,1,0:T(1,128)S(1)}, u32[]{:S(2)}, u32[]{:S(2)}) async-start(f32[64,1,128]{2,1,0:T(1,128)} %bitcast.5), calls=%async_computation | async-start | bytes 65536 | tf_op jit(solution)/shard_map/all_to_all | solution.py:671
  25.6 0.0 collective-permute-done.2.far
  25.6 0.1 outer.1
  25.7 1.3 %collective-permute-start.3 = (f32[24,8,256]{2,1,0:T(8,128)S(1)}, f32[24,8,256]{2,1,0:T(8,128)S(1)}, u32[]{:S(2)}, u32[]{:S(2)}) collective-permute-start(f32[24,8,256]{2,1,0:T(8,128)S(1)} %get-tuple-element.48), channel_id=1, source_target_pairs={{64,0},{128,64},{192,128},{65,1},{129,65},{193,129},{66,2},{130,66... | collective-permute-start | bytes 589832 | tf_op jit(solution)/shard_map/ppermute | solution.py:686
  27.0 4.0 %collective-permute-start.4 = (f32[4,3,8,256]{3,2,1,0:T(8,128)S(1)}, f32[4,3,8,256]{3,2,1,0:T(8,128)S(1)}, u32[]{:S(2)}, u32[]{:S(2)}) collective-permute-start(f32[4,3,8,256]{3,2,1,0:T(8,128)S(1)} %get-tuple-element.55), channel_id=1, source_target_pairs={{0,64},{64,128},{128,192},{1,65},{65,129},{129,193},{2,66},{66,130... | collective-permute-start | bytes 294920 | tf_op jit(solution)/shard_map/ppermute | solution.py:685
  31.0 3.9 %all-to-all-done = f32[64,1,128]{2,1,0:T(1,128)S(1)} async-done(((f32[64,1,128]{2,1,0:T(1,128)}), f32[64,1,128]{2,1,0:T(1,128)S(1)}, u32[]{:S(2)}, u32[]{:S(2)}) %all-to-all-start) | async-done | bytes 32800 | tf_op jit(solution)/shard_map/all_to_all | solution.py:671
  34.9 2.1 %fields.1 = (f32[2,4,256]{2,1,0:T(4,128)S(1)}, f32[132,8,256]{2,1,0:T(8,128)S(1)}, f32[8,3,8,256]{3,2,1,0:T(8,128)S(1)}, f32[8,3,8,256]{3,2,1,0:T(8,128)S(1)}) custom-call(f32[8,3,8,256]{3,2,1,0:T(8,128)} %bitcast.13, f32[8,3,8,256]{3,2,1,0:T(8,128)} %bitcast.16, f32[8,3,8,256]{3,2,1,0:T(8,128)} %bitcast.15, f32[64,128]{1,0:T(8,128)S(1)} %bitcast.10, ...), custom_call_target="tpu_custom_call" | custom-call | flops 2000000000 | bytes 6000000 | tf_op jit(solution)/shard_map/fields/pallas_call | solution.py:687
  37.0 0.0 collective-permute-done.3.outer
  37.0 1.1 %adjoint.1.image = f32[8,3,8,256]{3,2,1,0:T(8,128)S(1)} custom-call(f32[8,3,8,256]{3,2,1,0:T(8,128)S(1)} %get-tuple-element.47.mult, f32[24,8,256]{2,1,0:T(8,128)S(1)} %collective-permute-done.3.outer, f32[24,8,256]{2,1,0:T(8,128)S(1)} %get-tuple-element.49.mine, f32[2,2,8,256]{3,2,1,0:T(8,128)S(1)} %get-tuple-element.50.outermost, ...), custom_call_target="tpu_custom_call" | custom-call | flops 30000001024 | bytes 90000000 | tf_op jit(solution)/shard_map/adjoint/pallas_call | solution.py:702
  38.1 0.0 collective-permute-done.4.incoming
  38.1 0.8 %finish.1 = (f32[8,3,8,256]{3,2,1,0:T(8,128)}, f32[2,4,256]{2,1,0:T(4,128)}, f32[8,3,8,256]{3,2,1,0:T(8,128)}) custom-call(f32[8,3,8,256]{3,2,1,0:T(8,128)S(1)} %adjoint.1.image, f32[2,4,256]{2,1,0:T(4,128)S(1)} %get-tuple-element.53.report, f32[8,3,8,256]{3,2,1,0:T(8,128)S(1)} %get-tuple-element.54.model, f32[4,3,8,256]{3,2,1,0:T(8,128)S(1)} %collective-permute-done.4.incoming), custom_call_target="tpu_custom_call" | custom-call | tf_op jit(solution)/shard_map/finish/pallas_call | solution.py:715
Async XLA Ops:
  2.0 10.0 %collective-permute-start = (f32[38,8,256]{2,1,0:T(8,128)S(1)}, f32[38,8,256]{2,1,0:T(8,128)S(1)}, u32[]{:S(2)}, u32[]{:S(2)}) collective-permute-start(f32[38,8,256]{2,1,0:T(8,128)S(1)} %get-tuple-element.39), channel_id=1, source_target_pairs={{0,1},{2,3},{4,5},{6,7},{8,9},{10,11},{12,13},{14,15},{16,17},{18,... | collective-permute-start | bytes 933896 | tf_op jit(solution)/shard_map/ppermute | solution.py:631
  5.3 6.7 %collective-permute-start.1 = (f32[21,8,256]{2,1,0:T(8,128)S(1)}, f32[21,8,256]{2,1,0:T(8,128)S(1)}, u32[]{:S(2)}, u32[]{:S(2)}) collective-permute-start(f32[21,8,256]{2,1,0:T(8,128)S(1)} %get-tuple-element.40), channel_id=1, source_target_pairs={{1,2},{3,4},{5,6},{7,8},{9,10},{11,12},{13,14},{15,16},{17,18},{19... | collective-permute-start | bytes 516104 | tf_op jit(solution)/shard_map/ppermute | solution.py:630
  7.3 4.8 %copy-start = (f32[2,4,256]{2,1,0:T(4,128)S(1)}, f32[2,4,256]{2,1,0:T(4,128)}, u32[]{:S(2)}) copy-start(f32[2,4,256]{2,1,0:T(4,128)} %owned.1) | copy-start | bytes 24580
  7.3 4.8 %copy-start.1 = (f32[2,4,256]{2,1,0:T(4,128)S(1)}, f32[2,4,256]{2,1,0:T(4,128)}, u32[]{:S(2)}) copy-start(f32[2,4,256]{2,1,0:T(4,128)} %owned_variance.1) | copy-start | bytes 24580
  8.4 17.2 %collective-permute-start.2 = (f32[17,8,256]{2,1,0:T(8,128)S(1)}, f32[17,8,256]{2,1,0:T(8,128)S(1)}, u32[]{:S(2)}, u32[]{:S(2)}) collective-permute-start(f32[17,8,256]{2,1,0:T(8,128)S(1)} %get-tuple-element.43), channel_id=1, source_target_pairs={{1,2},{3,4},{5,6},{7,8},{9,10},{11,12},{13,14},{15,16},{17,18},{19... | collective-permute-start | bytes 417800 | tf_op jit(solution)/shard_map/ppermute | solution.py:645
  13.9 21.0 %all-to-all-start = ((f32[64,1,128]{2,1,0:T(1,128)}), f32[64,1,128]{2,1,0:T(1,128)S(1)}, u32[]{:S(2)}, u32[]{:S(2)}) async-start(f32[64,1,128]{2,1,0:T(1,128)} %bitcast.5), calls=%async_computation | async-start | bytes 65536 | tf_op jit(solution)/shard_map/all_to_all | solution.py:671
  25.7 11.3 %collective-permute-start.3 = (f32[24,8,256]{2,1,0:T(8,128)S(1)}, f32[24,8,256]{2,1,0:T(8,128)S(1)}, u32[]{:S(2)}, u32[]{:S(2)}) collective-permute-start(f32[24,8,256]{2,1,0:T(8,128)S(1)} %get-tuple-element.48), channel_id=1, source_target_pairs={{64,0},{128,64},{192,128},{65,1},{129,65},{193,129},{66,2},{130,66... | collective-permute-start | bytes 589832 | tf_op jit(solution)/shard_map/ppermute | solution.py:686
  27.0 11.1 %collective-permute-start.4 = (f32[4,3,8,256]{3,2,1,0:T(8,128)S(1)}, f32[4,3,8,256]{3,2,1,0:T(8,128)S(1)}, u32[]{:S(2)}, u32[]{:S(2)}) collective-permute-start(f32[4,3,8,256]{3,2,1,0:T(8,128)S(1)} %get-tuple-element.55), channel_id=1, source_target_pairs={{0,64},{64,128},{128,192},{1,65},{65,129},{129,193},{2,66},{66,130... | collective-permute-start | bytes 294920 | tf_op jit(solution)/shard_map/ppermute | solution.py:685
where the time goes:
time: 39.1 us; the launch traced here: 38.9 us
  starting transfers between devices  25.9 us (66%)
  Pallas kernels  8.28 us (21%)
  waiting for transfers between devices  3.96 us (10%)
  between operations  0.76 us (2%)
    all_to_all x1, starting transfers between devices, per_device(): got = lax.all_to_all(send, 'space', split_axis=0, concat_axis=0, tiled=True)  11.7 us
    ppermute x1, starting transfers between devices, per_device(): lax.ppermute(final1, 'win', [(i, i + 1) for i in range(wins - 1)])  3.99 us
    all_to_all x1, waiting for transfers between devices, per_device(): got = lax.all_to_all(send, 'space', split_axis=0, concat_axis=0, tiled=True)  3.93 us
    ppermute x1, starting transfers between devices, per_device(): lax.ppermute(far, 'space', both([(i, i + 1) for i in range(1, count - 1,...  3.64 us
    ppermute x1, starting transfers between devices, per_device(): lax.ppermute(inner, 'space', both([(i, i + 1) for i in range(0, count, 2)]))  3.33 us
    pallas_call x1, Pallas kernels, per_device(): pl.pallas_call(fields_kernel, name='fields', out_shape=(shaped(2, STEPS,...  2.06 us
    ppermute x1, starting transfers between devices, per_device(): lax.ppermute(near, 'space', both([(i, i + 1) for i in range(1, count - 1,...  1.91 us
    pallas_call x1, Pallas kernels, per_device(): pl.pallas_call(tangent_kernel, name='tangent', out_shape=(shaped(LEVELS,...  1.8 us
  transfers between devices with their start and end apart: 6, of which 1 were waited for; matrix products, arithmetic and copies ran while one was open for 0% of the time, Pallas kernels for 16%

commit v1 on v0

--- a/solution.py
+++ b/solution.py
@@ -101,8 +101,9 @@
 
 
 def one_hot_columns(column):
-    place = lax.broadcasted_iota(jnp.int32, (NX, NX), 0)
-    return jnp.where(place == column, 1.0, 0.0).astype(f32).astype(bf16)
+    place = lax.broadcasted_iota(jnp.int32, (NX, NX), 0).astype(jnp.int16)
+    here = place == jnp.broadcast_to(column, (NX, NX)).astype(jnp.int16)
+    return jnp.where(here, jnp.ones((NX, NX), bf16), jnp.zeros((NX, NX), bf16))
 
 
 def lower_half():

time: 39.1 us -> 38.8 us (level)
  transfers between devices with their start and end apart: 6 -> 6, of which waited for: 1 -> 1; matrix products, arithmetic and copies ran while one was open for 0% -> 0% of each run, Pallas kernels for 16% -> 15%
where the time goes in v1:
time: 38.8 us; the launch traced here: 38.6 us
  starting transfers between devices  25.9 us (67%)
  Pallas kernels  7.97 us (21%)
  waiting for transfers between devices  3.96 us (10%)
  between operations  0.76 us (2%)
    all_to_all x1, starting transfers between devices, per_device(): got = lax.all_to_all(send, 'space', split_axis=0, concat_axis=0, tiled=True)  11.7 us
    ppermute x1, starting transfers between devices, per_device(): lax.ppermute(final1, 'win', [(i, i + 1) for i in range(wins - 1)])  3.99 us
    all_to_all x1, waiting for transfers between devices, per_device(): got = lax.all_to_all(send, 'space', split_axis=0, concat_axis=0, tiled=True)  3.93 us
    ppermute x1, starting transfers between devices, per_device(): lax.ppermute(far, 'space', both([(i, i + 1) for i in range(1, count - 1,...  3.64 us
    ppermute x1, starting transfers between devices, per_device(): lax.ppermute(inner, 'space', both([(i, i + 1) for i in range(0, count, 2)]))  3.33 us
    ppermute x1, starting transfers between devices, per_device(): lax.ppermute(near, 'space', both([(i, i + 1) for i in range(1, count - 1,...  1.91 us
    pallas_call x1, Pallas kernels, per_device(): pl.pallas_call(tangent_kernel, name='tangent', out_shape=(shaped(LEVELS,...  1.8 us
    pallas_call x1, Pallas kernels, per_device(): pl.pallas_call(fields_kernel, name='fields', out_shape=(shaped(2, STEPS,...  1.75 us
  transfers between devices with their start and end apart: 6, of which 1 were waited for; matrix products, arithmetic and copies ran while one was open for 0% of the time, Pallas kernels for 15%

profile of v1, /device:TPU:1, one launch (start us, length us, event | category | flops | bytes accessed | tf_op | source)
XLA Modules:
  0.0 38.6 jit_solution(12930615786404301472)
XLA Ops:
  0.6 1.4 %pack.1 = (f32[21,8,256]{2,1,0:T(8,128)S(1)}, f32[38,8,256]{2,1,0:T(8,128)S(1)}, f32[3,8,256]{2,1,0:T(8,128)S(1)}, f32[3,8,8,256]{3,2,1,0:T(8,128)S(1)}, f32[3,8...) custom-call(f32[8,3,8,256]{3,2,1,0:T(8,128)} %bitcast.14, f32[8,3,8,256]{3,2,1,0:T(8,128)} %bitcast.11, ...), custom_call_target="tpu_custom_call" | custom-call | tf_op jit(solution)/shard_map/pack/pallas_call | solution.py:603
  2.0 3.3 %collective-permute-start = (f32[38,8,256]{2,1,0:T(8,128)S(1)}, f32[38,8,256]{2,1,0:T(8,128)S(1)}, u32[]{:S(2)}, u32[]{:S(2)}) collective-permute-start(f32[38,8,256]{2,1,0:T(8,128)S(1)} %get-tuple-element.39), channel_id=1, source_target_pairs={{0,1},{2,3},{4,5},{6,7},{8,9},{10,11},{12,13},{14,15},{16,17},{18,... | collective-permute-start | bytes 933896 | tf_op jit(solution)/shard_map/ppermute | solution.py:632
  5.3 1.9 %collective-permute-start.1 = (f32[21,8,256]{2,1,0:T(8,128)S(1)}, f32[21,8,256]{2,1,0:T(8,128)S(1)}, u32[]{:S(2)}, u32[]{:S(2)}) collective-permute-start(f32[21,8,256]{2,1,0:T(8,128)S(1)} %get-tuple-element.40), channel_id=1, source_target_pairs={{1,2},{3,4},{5,6},{7,8},{9,10},{11,12},{13,14},{15,16},{17,18},{19... | collective-permute-start | bytes 516104 | tf_op jit(solution)/shard_map/ppermute | solution.py:631
  7.3 0.0 copy-start
  7.3 0.0 copy-start.1
  7.3 1.1 %prepare.1 = (f32[17,8,256]{2,1,0:T(8,128)S(1)}, bf16[8,256,256]{2,1,0:T(8,128)(2,1)S(1)}, bf16[8,256,256]{2,1,0:T(8,128)(2,1)S(1)}, f32[8,256]{1,0:T(8,128)S(1)}, f32[3,3,8,8,256]{4,3,2,1,0:T(8,128)S(1)}) custom-call(f32[3,8,8,256]{3,2,1,0:T(8,128)S(1)} %get-tuple-element.31.inc_rows, f32[3,8,8,256]{3,2,1,0:T(8,128)S(1)} %get-tuple-element.32.bg_rows, ...), custom_call_target="tpu_custom_call" | custom-call | flops 2000000000 | bytes 6000000 | tf_op jit(solution)/shard_map/prepare/pallas_call | solution.py:634
  8.4 3.6 %collective-permute-start.2 = (f32[17,8,256]{2,1,0:T(8,128)S(1)}, f32[17,8,256]{2,1,0:T(8,128)S(1)}, u32[]{:S(2)}, u32[]{:S(2)}) collective-permute-start(f32[17,8,256]{2,1,0:T(8,128)S(1)} %get-tuple-element.43), channel_id=1, source_target_pairs={{1,2},{3,4},{5,6},{7,8},{9,10},{11,12},{13,14},{15,16},{17,18},{19... | collective-permute-start | bytes 417800 | tf_op jit(solution)/shard_map/ppermute | solution.py:646
  12.0 0.0 collective-permute-done.1.got_near
  12.1 0.0 collective-permute-done.got_a.inner
  12.1 0.0 copy-done
  12.1 0.0 copy-done.1
  12.1 1.8 %tangent.1 = (f32[4,3,8,256]{3,2,1,0:T(8,128)S(1)}, f32[4,3,8,256]{3,2,1,0:T(8,128)S(1)}, f32[64,128]{1,0:T(8,128)}, f32[8,256]{1,0:T(8,128)S(1)}, f32[3,16,8,256]{3,2,1,0:T(8,128)S(1)}) custom-call(f32[3,8,8,256]{3,2,1,0:T(8,128)S(1)} %get-tuple-element.31.inc_rows, f32[3,8,8,256]{3,2,1,0:T(8,128)S(1)} %get-tuple-element.32.bg_rows, ...), custom_call_target="tpu_custom_call" | custom-call | flops 2000000000 | bytes 6000000 | tf_op jit(solution)/shard_map/tangent/pallas_call | solution.py:647
  13.9 11.7 %all-to-all-start = ((f32[64,1,128]{2,1,0:T(1,128)}), f32[64,1,128]{2,1,0:T(1,128)S(1)}, u32[]{:S(2)}, u32[]{:S(2)}) async-start(f32[64,1,128]{2,1,0:T(1,128)} %bitcast.5), calls=%async_computation | async-start | bytes 65536 | tf_op jit(solution)/shard_map/all_to_all | solution.py:672
  25.6 0.0 collective-permute-done.2.far
  25.6 0.1 outer.1
  25.7 1.3 %collective-permute-start.3 = (f32[24,8,256]{2,1,0:T(8,128)S(1)}, f32[24,8,256]{2,1,0:T(8,128)S(1)}, u32[]{:S(2)}, u32[]{:S(2)}) collective-permute-start(f32[24,8,256]{2,1,0:T(8,128)S(1)} %get-tuple-element.48), channel_id=1, source_target_pairs={{64,0},{128,64},{192,128},{65,1},{129,65},{193,129},{66,2},{130,66... | collective-permute-start | bytes 589832 | tf_op jit(solution)/shard_map/ppermute | solution.py:687
  27.0 4.0 %collective-permute-start.4 = (f32[4,3,8,256]{3,2,1,0:T(8,128)S(1)}, f32[4,3,8,256]{3,2,1,0:T(8,128)S(1)}, u32[]{:S(2)}, u32[]{:S(2)}) collective-permute-start(f32[4,3,8,256]{3,2,1,0:T(8,128)S(1)} %get-tuple-element.55), channel_id=1, source_target_pairs={{0,64},{64,128},{128,192},{1,65},{65,129},{129,193},{2,66},{66,130... | collective-permute-start | bytes 294920 | tf_op jit(solution)/shard_map/ppermute | solution.py:686
  31.0 3.9 %all-to-all-done = f32[64,1,128]{2,1,0:T(1,128)S(1)} async-done(((f32[64,1,128]{2,1,0:T(1,128)}), f32[64,1,128]{2,1,0:T(1,128)S(1)}, u32[]{:S(2)}, u32[]{:S(2)}) %all-to-all-start) | async-done | bytes 32800 | tf_op jit(solution)/shard_map/all_to_all | solution.py:672
  34.9 1.7 %fields.1 = (f32[2,4,256]{2,1,0:T(4,128)S(1)}, f32[132,8,256]{2,1,0:T(8,128)S(1)}, f32[8,3,8,256]{3,2,1,0:T(8,128)S(1)}, f32[8,3,8,256]{3,2,1,0:T(8,128)S(1)}) custom-call(f32[8,3,8,256]{3,2,1,0:T(8,128)} %bitcast.13, f32[8,3,8,256]{3,2,1,0:T(8,128)} %bitcast.16, f32[8,3,8,256]{3,2,1,0:T(8,128)} %bitcast.15, f32[64,128]{1,0:T(8,128)S(1)} %bitcast.10, ...), custom_call_target="tpu_custom_call" | custom-call | flops 2000000000 | bytes 6000000 | tf_op jit(solution)/shard_map/fields/pallas_call | solution.py:688
  36.7 0.0 collective-permute-done.3.outer
  36.7 1.1 %adjoint.1.image = f32[8,3,8,256]{3,2,1,0:T(8,128)S(1)} custom-call(f32[8,3,8,256]{3,2,1,0:T(8,128)S(1)} %get-tuple-element.47.mult, f32[24,8,256]{2,1,0:T(8,128)S(1)} %collective-permute-done.3.outer, f32[24,8,256]{2,1,0:T(8,128)S(1)} %get-tuple-element.49.mine, f32[2,2,8,256]{3,2,1,0:T(8,128)S(1)} %get-tuple-element.50.outermost, ...), custom_call_target="tpu_custom_call" | custom-call | flops 30000001024 | bytes 90000000 | tf_op jit(solution)/shard_map/adjoint/pallas_call | solution.py:703
  37.8 0.0 collective-permute-done.4.incoming
  37.8 0.8 %finish.1 = (f32[8,3,8,256]{3,2,1,0:T(8,128)}, f32[2,4,256]{2,1,0:T(4,128)}, f32[8,3,8,256]{3,2,1,0:T(8,128)}) custom-call(f32[8,3,8,256]{3,2,1,0:T(8,128)S(1)} %adjoint.1.image, f32[2,4,256]{2,1,0:T(4,128)S(1)} %get-tuple-element.53.report, f32[8,3,8,256]{3,2,1,0:T(8,128)S(1)} %get-tuple-element.54.model, f32[4,3,8,256]{3,2,1,0:T(8,128)S(1)} %collective-permute-done.4.incoming), custom_call_target="tpu_custom_call" | custom-call | tf_op jit(solution)/shard_map/finish/pallas_call | solution.py:716
Async XLA Ops:
  2.0 10.0 %collective-permute-start = (f32[38,8,256]{2,1,0:T(8,128)S(1)}, f32[38,8,256]{2,1,0:T(8,128)S(1)}, u32[]{:S(2)}, u32[]{:S(2)}) collective-permute-start(f32[38,8,256]{2,1,0:T(8,128)S(1)} %get-tuple-element.39), channel_id=1, source_target_pairs={{0,1},{2,3},{4,5},{6,7},{8,9},{10,11},{12,13},{14,15},{16,17},{18,... | collective-permute-start | bytes 933896 | tf_op jit(solution)/shard_map/ppermute | solution.py:632
  5.3 6.7 %collective-permute-start.1 = (f32[21,8,256]{2,1,0:T(8,128)S(1)}, f32[21,8,256]{2,1,0:T(8,128)S(1)}, u32[]{:S(2)}, u32[]{:S(2)}) collective-permute-start(f32[21,8,256]{2,1,0:T(8,128)S(1)} %get-tuple-element.40), channel_id=1, source_target_pairs={{1,2},{3,4},{5,6},{7,8},{9,10},{11,12},{13,14},{15,16},{17,18},{19... | collective-permute-start | bytes 516104 | tf_op jit(solution)/shard_map/ppermute | solution.py:631
  7.3 4.8 %copy-start = (f32[2,4,256]{2,1,0:T(4,128)S(1)}, f32[2,4,256]{2,1,0:T(4,128)}, u32[]{:S(2)}) copy-start(f32[2,4,256]{2,1,0:T(4,128)} %owned.1) | copy-start | bytes 24580
  7.3 4.8 %copy-start.1 = (f32[2,4,256]{2,1,0:T(4,128)S(1)}, f32[2,4,256]{2,1,0:T(4,128)}, u32[]{:S(2)}) copy-start(f32[2,4,256]{2,1,0:T(4,128)} %owned_variance.1) | copy-start | bytes 24580
  8.4 17.2 %collective-permute-start.2 = (f32[17,8,256]{2,1,0:T(8,128)S(1)}, f32[17,8,256]{2,1,0:T(8,128)S(1)}, u32[]{:S(2)}, u32[]{:S(2)}) collective-permute-start(f32[17,8,256]{2,1,0:T(8,128)S(1)} %get-tuple-element.43), channel_id=1, source_target_pairs={{1,2},{3,4},{5,6},{7,8},{9,10},{11,12},{13,14},{15,16},{17,18},{19... | collective-permute-start | bytes 417800 | tf_op jit(solution)/shard_map/ppermute | solution.py:646
  13.9 21.0 %all-to-all-start = ((f32[64,1,128]{2,1,0:T(1,128)}), f32[64,1,128]{2,1,0:T(1,128)S(1)}, u32[]{:S(2)}, u32[]{:S(2)}) async-start(f32[64,1,128]{2,1,0:T(1,128)} %bitcast.5), calls=%async_computation | async-start | bytes 65536 | tf_op jit(solution)/shard_map/all_to_all | solution.py:672
  25.7 11.0 %collective-permute-start.3 = (f32[24,8,256]{2,1,0:T(8,128)S(1)}, f32[24,8,256]{2,1,0:T(8,128)S(1)}, u32[]{:S(2)}, u32[]{:S(2)}) collective-permute-start(f32[24,8,256]{2,1,0:T(8,128)S(1)} %get-tuple-element.48), channel_id=1, source_target_pairs={{64,0},{128,64},{192,128},{65,1},{129,65},{193,129},{66,2},{130,66... | collective-permute-start | bytes 589832 | tf_op jit(solution)/shard_map/ppermute | solution.py:687
  27.0 10.8 %collective-permute-start.4 = (f32[4,3,8,256]{3,2,1,0:T(8,128)S(1)}, f32[4,3,8,256]{3,2,1,0:T(8,128)S(1)}, u32[]{:S(2)}, u32[]{:S(2)}) collective-permute-start(f32[4,3,8,256]{3,2,1,0:T(8,128)S(1)} %get-tuple-element.55), channel_id=1, source_target_pairs={{0,64},{64,128},{128,192},{1,65},{65,129},{129,193},{2,66},{66,130... | collective-permute-start | bytes 294920 | tf_op jit(solution)/shard_map/ppermute | solution.py:686

commit v2 on v1

--- a/solution.py
+++ b/solution.py
@@ -95,9 +95,20 @@
 def column_weights(report, n):
     _, column = decode(report[0, n : n + 1])
     share = report[1, n : n + 1]
-    place = lax.broadcasted_iota(jnp.int32, (NX, NX), 0)
-    following = jnp.where(place == ((column + 1) & (NX - 1)), share, 0.0)
-    return split(jnp.where(place == column, 1.0 - share, following))
+    place = lax.broadcasted_iota(jnp.int32, (NX, NX), 0).astype(jnp.int16)
+
+    def spread(row, kind):
+        return jnp.broadcast_to(row, (NX, NX)).astype(kind)
+
+    here = place == spread(column, jnp.int16)
+    following = place == spread((column + 1) & (NX - 1), jnp.int16)
+    none = jnp.zeros((NX, NX), bf16)
+    return [
+        jnp.where(here, spread(own, bf16), jnp.where(following, spread(other, bf16), none))
+        for own, other in zip(
+            (x.astype(f32) for x in split(1.0 - share)), (x.astype(f32) for x in split(share))
+        )
+    ]
 
 
 def one_hot_columns(column):

time: 38.8 us -> 38.8 us (level)
  transfers between devices with their start and end apart: 6 -> 6, of which waited for: 1 -> 2; matrix products, arithmetic and copies ran while one was open for 0% -> 0% of each run, Pallas kernels for 15% -> 14%
where the time goes in v2:
time: 38.8 us; the launch traced here: 38.6 us
  starting transfers between devices  25.9 us (67%)
  Pallas kernels  7.68 us (20%)
  waiting for transfers between devices  4.25 us (11%)
  between operations  0.75 us (2%)
    all_to_all x1, starting transfers between devices, per_device(): got = lax.all_to_all(send, 'space', split_axis=0, concat_axis=0, tiled=True)  11.7 us
    ppermute x1, starting transfers between devices, per_device(): lax.ppermute(final1, 'win', [(i, i + 1) for i in range(wins - 1)])  3.99 us
    all_to_all x1, waiting for transfers between devices, per_device(): got = lax.all_to_all(send, 'space', split_axis=0, concat_axis=0, tiled=True)  3.93 us
    ppermute x1, starting transfers between devices, per_device(): lax.ppermute(far, 'space', both([(i, i + 1) for i in range(1, count - 1,...  3.64 us
    ppermute x1, starting transfers between devices, per_device(): lax.ppermute(inner, 'space', both([(i, i + 1) for i in range(0, count, 2)]))  3.33 us
    ppermute x1, starting transfers between devices, per_device(): lax.ppermute(near, 'space', both([(i, i + 1) for i in range(1, count - 1,...  1.91 us
    pallas_call x1, Pallas kernels, per_device(): pl.pallas_call(tangent_kernel, name='tangent', out_shape=(shaped(LEVELS,...  1.81 us
    pallas_call x1, Pallas kernels, per_device(): pl.pallas_call(fields_kernel, name='fields', out_shape=(shaped(2, STEPS,...  1.75 us
  transfers between devices with their start and end apart: 6, of which 2 were waited for; matrix products, arithmetic and copies ran while one was open for 0% of the time, Pallas kernels for 14%

profile of v2, /device:TPU:1, one launch (start us, length us, event | category | flops | bytes accessed | tf_op | source)
XLA Modules:
  0.0 38.6 jit_solution(4127424923116991655)
XLA Ops:
  0.6 1.4 %pack.1 = (f32[21,8,256]{2,1,0:T(8,128)S(1)}, f32[38,8,256]{2,1,0:T(8,128)S(1)}, f32[3,8,256]{2,1,0:T(8,128)S(1)}, f32[3,8,8,256]{3,2,1,0:T(8,128)S(1)}, f32[3,8...) custom-call(f32[8,3,8,256]{3,2,1,0:T(8,128)} %bitcast.14, f32[8,3,8,256]{3,2,1,0:T(8,128)} %bitcast.11, ...), custom_call_target="tpu_custom_call" | custom-call | tf_op jit(solution)/shard_map/pack/pallas_call | solution.py:614
  2.0 3.3 %collective-permute-start = (f32[38,8,256]{2,1,0:T(8,128)S(1)}, f32[38,8,256]{2,1,0:T(8,128)S(1)}, u32[]{:S(2)}, u32[]{:S(2)}) collective-permute-start(f32[38,8,256]{2,1,0:T(8,128)S(1)} %get-tuple-element.39), channel_id=1, source_target_pairs={{0,1},{2,3},{4,5},{6,7},{8,9},{10,11},{12,13},{14,15},{16,17},{18,... | collective-permute-start | bytes 933896 | tf_op jit(solution)/shard_map/ppermute | solution.py:643
  5.3 1.9 %collective-permute-start.1 = (f32[21,8,256]{2,1,0:T(8,128)S(1)}, f32[21,8,256]{2,1,0:T(8,128)S(1)}, u32[]{:S(2)}, u32[]{:S(2)}) collective-permute-start(f32[21,8,256]{2,1,0:T(8,128)S(1)} %get-tuple-element.40), channel_id=1, source_target_pairs={{1,2},{3,4},{5,6},{7,8},{9,10},{11,12},{13,14},{15,16},{17,18},{19... | collective-permute-start | bytes 516104 | tf_op jit(solution)/shard_map/ppermute | solution.py:642
  7.3 0.0 copy-start
  7.3 0.0 copy-start.1
  7.3 0.8 %prepare.1 = (f32[17,8,256]{2,1,0:T(8,128)S(1)}, bf16[8,256,256]{2,1,0:T(8,128)(2,1)S(1)}, bf16[8,256,256]{2,1,0:T(8,128)(2,1)S(1)}, f32[8,256]{1,0:T(8,128)S(1)}, f32[3,3,8,8,256]{4,3,2,1,0:T(8,128)S(1)}) custom-call(f32[3,8,8,256]{3,2,1,0:T(8,128)S(1)} %get-tuple-element.31.inc_rows, f32[3,8,8,256]{3,2,1,0:T(8,128)S(1)} %get-tuple-element.32.bg_rows, ...), custom_call_target="tpu_custom_call" | custom-call | flops 2000000000 | bytes 6000000 | tf_op jit(solution)/shard_map/prepare/pallas_call | solution.py:645
  8.1 3.6 %collective-permute-start.2 = (f32[17,8,256]{2,1,0:T(8,128)S(1)}, f32[17,8,256]{2,1,0:T(8,128)S(1)}, u32[]{:S(2)}, u32[]{:S(2)}) collective-permute-start(f32[17,8,256]{2,1,0:T(8,128)S(1)} %get-tuple-element.43), channel_id=1, source_target_pairs={{1,2},{3,4},{5,6},{7,8},{9,10},{11,12},{13,14},{15,16},{17,18},{19... | collective-permute-start | bytes 417800 | tf_op jit(solution)/shard_map/ppermute | solution.py:657
  11.8 0.3 collective-permute-done.1.got_near
  12.1 0.0 collective-permute-done.got_a.inner
  12.1 0.0 copy-done
  12.1 0.0 copy-done.1
  12.1 1.8 %tangent.1 = (f32[4,3,8,256]{3,2,1,0:T(8,128)S(1)}, f32[4,3,8,256]{3,2,1,0:T(8,128)S(1)}, f32[64,128]{1,0:T(8,128)}, f32[8,256]{1,0:T(8,128)S(1)}, f32[3,16,8,256]{3,2,1,0:T(8,128)S(1)}) custom-call(f32[3,8,8,256]{3,2,1,0:T(8,128)S(1)} %get-tuple-element.31.inc_rows, f32[3,8,8,256]{3,2,1,0:T(8,128)S(1)} %get-tuple-element.32.bg_rows, ...), custom_call_target="tpu_custom_call" | custom-call | flops 2000000000 | bytes 6000000 | tf_op jit(solution)/shard_map/tangent/pallas_call | solution.py:658
  13.9 11.7 %all-to-all-start = ((f32[64,1,128]{2,1,0:T(1,128)}), f32[64,1,128]{2,1,0:T(1,128)S(1)}, u32[]{:S(2)}, u32[]{:S(2)}) async-start(f32[64,1,128]{2,1,0:T(1,128)} %bitcast.5), calls=%async_computation | async-start | bytes 65536 | tf_op jit(solution)/shard_map/all_to_all | solution.py:683
  25.6 0.0 collective-permute-done.2.far
  25.6 0.1 outer.1
  25.7 1.3 %collective-permute-start.3 = (f32[24,8,256]{2,1,0:T(8,128)S(1)}, f32[24,8,256]{2,1,0:T(8,128)S(1)}, u32[]{:S(2)}, u32[]{:S(2)}) collective-permute-start(f32[24,8,256]{2,1,0:T(8,128)S(1)} %get-tuple-element.48), channel_id=1, source_target_pairs={{64,0},{128,64},{192,128},{65,1},{129,65},{193,129},{66,2},{130,66... | collective-permute-start | bytes 589832 | tf_op jit(solution)/shard_map/ppermute | solution.py:698
  27.0 4.0 %collective-permute-start.4 = (f32[4,3,8,256]{3,2,1,0:T(8,128)S(1)}, f32[4,3,8,256]{3,2,1,0:T(8,128)S(1)}, u32[]{:S(2)}, u32[]{:S(2)}) collective-permute-start(f32[4,3,8,256]{3,2,1,0:T(8,128)S(1)} %get-tuple-element.55), channel_id=1, source_target_pairs={{0,64},{64,128},{128,192},{1,65},{65,129},{129,193},{2,66},{66,130... | collective-permute-start | bytes 294920 | tf_op jit(solution)/shard_map/ppermute | solution.py:697
  31.0 3.9 %all-to-all-done = f32[64,1,128]{2,1,0:T(1,128)S(1)} async-done(((f32[64,1,128]{2,1,0:T(1,128)}), f32[64,1,128]{2,1,0:T(1,128)S(1)}, u32[]{:S(2)}, u32[]{:S(2)}) %all-to-all-start) | async-done | bytes 32800 | tf_op jit(solution)/shard_map/all_to_all | solution.py:683
  34.9 1.7 %fields.1 = (f32[2,4,256]{2,1,0:T(4,128)S(1)}, f32[132,8,256]{2,1,0:T(8,128)S(1)}, f32[8,3,8,256]{3,2,1,0:T(8,128)S(1)}, f32[8,3,8,256]{3,2,1,0:T(8,128)S(1)}) custom-call(f32[8,3,8,256]{3,2,1,0:T(8,128)} %bitcast.13, f32[8,3,8,256]{3,2,1,0:T(8,128)} %bitcast.16, f32[8,3,8,256]{3,2,1,0:T(8,128)} %bitcast.15, f32[64,128]{1,0:T(8,128)S(1)} %bitcast.10, ...), custom_call_target="tpu_custom_call" | custom-call | flops 2000000000 | bytes 6000000 | tf_op jit(solution)/shard_map/fields/pallas_call | solution.py:699
  36.7 0.0 collective-permute-done.3.outer
  36.7 1.1 %adjoint.1.image = f32[8,3,8,256]{3,2,1,0:T(8,128)S(1)} custom-call(f32[8,3,8,256]{3,2,1,0:T(8,128)S(1)} %get-tuple-element.47.mult, f32[24,8,256]{2,1,0:T(8,128)S(1)} %collective-permute-done.3.outer, f32[24,8,256]{2,1,0:T(8,128)S(1)} %get-tuple-element.49.mine, f32[2,2,8,256]{3,2,1,0:T(8,128)S(1)} %get-tuple-element.50.outermost, ...), custom_call_target="tpu_custom_call" | custom-call | flops 30000001024 | bytes 90000000 | tf_op jit(solution)/shard_map/adjoint/pallas_call | solution.py:714
  37.8 0.0 collective-permute-done.4.incoming
  37.8 0.8 %finish.1 = (f32[8,3,8,256]{3,2,1,0:T(8,128)}, f32[2,4,256]{2,1,0:T(4,128)}, f32[8,3,8,256]{3,2,1,0:T(8,128)}) custom-call(f32[8,3,8,256]{3,2,1,0:T(8,128)S(1)} %adjoint.1.image, f32[2,4,256]{2,1,0:T(4,128)S(1)} %get-tuple-element.53.report, f32[8,3,8,256]{3,2,1,0:T(8,128)S(1)} %get-tuple-element.54.model, f32[4,3,8,256]{3,2,1,0:T(8,128)S(1)} %collective-permute-done.4.incoming), custom_call_target="tpu_custom_call" | custom-call | tf_op jit(solution)/shard_map/finish/pallas_call | solution.py:727
Async XLA Ops:
  2.0 10.0 %collective-permute-start = (f32[38,8,256]{2,1,0:T(8,128)S(1)}, f32[38,8,256]{2,1,0:T(8,128)S(1)}, u32[]{:S(2)}, u32[]{:S(2)}) collective-permute-start(f32[38,8,256]{2,1,0:T(8,128)S(1)} %get-tuple-element.39), channel_id=1, source_target_pairs={{0,1},{2,3},{4,5},{6,7},{8,9},{10,11},{12,13},{14,15},{16,17},{18,... | collective-permute-start | bytes 933896 | tf_op jit(solution)/shard_map/ppermute | solution.py:643
  5.3 6.7 %collective-permute-start.1 = (f32[21,8,256]{2,1,0:T(8,128)S(1)}, f32[21,8,256]{2,1,0:T(8,128)S(1)}, u32[]{:S(2)}, u32[]{:S(2)}) collective-permute-start(f32[21,8,256]{2,1,0:T(8,128)S(1)} %get-tuple-element.40), channel_id=1, source_target_pairs={{1,2},{3,4},{5,6},{7,8},{9,10},{11,12},{13,14},{15,16},{17,18},{19... | collective-permute-start | bytes 516104 | tf_op jit(solution)/shard_map/ppermute | solution.py:642
  7.3 4.8 %copy-start = (f32[2,4,256]{2,1,0:T(4,128)S(1)}, f32[2,4,256]{2,1,0:T(4,128)}, u32[]{:S(2)}) copy-start(f32[2,4,256]{2,1,0:T(4,128)} %owned.1) | copy-start | bytes 24580
  7.3 4.8 %copy-start.1 = (f32[2,4,256]{2,1,0:T(4,128)S(1)}, f32[2,4,256]{2,1,0:T(4,128)}, u32[]{:S(2)}) copy-start(f32[2,4,256]{2,1,0:T(4,128)} %owned_variance.1) | copy-start | bytes 24580
  8.1 17.5 %collective-permute-start.2 = (f32[17,8,256]{2,1,0:T(8,128)S(1)}, f32[17,8,256]{2,1,0:T(8,128)S(1)}, u32[]{:S(2)}, u32[]{:S(2)}) collective-permute-start(f32[17,8,256]{2,1,0:T(8,128)S(1)} %get-tuple-element.43), channel_id=1, source_target_pairs={{1,2},{3,4},{5,6},{7,8},{9,10},{11,12},{13,14},{15,16},{17,18},{19... | collective-permute-start | bytes 417800 | tf_op jit(solution)/shard_map/ppermute | solution.py:657
  13.9 21.0 %all-to-all-start = ((f32[64,1,128]{2,1,0:T(1,128)}), f32[64,1,128]{2,1,0:T(1,128)S(1)}, u32[]{:S(2)}, u32[]{:S(2)}) async-start(f32[64,1,128]{2,1,0:T(1,128)} %bitcast.5), calls=%async_computation | async-start | bytes 65536 | tf_op jit(solution)/shard_map/all_to_all | solution.py:683
  25.7 11.0 %collective-permute-start.3 = (f32[24,8,256]{2,1,0:T(8,128)S(1)}, f32[24,8,256]{2,1,0:T(8,128)S(1)}, u32[]{:S(2)}, u32[]{:S(2)}) collective-permute-start(f32[24,8,256]{2,1,0:T(8,128)S(1)} %get-tuple-element.48), channel_id=1, source_target_pairs={{64,0},{128,64},{192,128},{65,1},{129,65},{193,129},{66,2},{130,66... | collective-permute-start | bytes 589832 | tf_op jit(solution)/shard_map/ppermute | solution.py:698
  27.0 10.8 %collective-permute-start.4 = (f32[4,3,8,256]{3,2,1,0:T(8,128)S(1)}, f32[4,3,8,256]{3,2,1,0:T(8,128)S(1)}, u32[]{:S(2)}, u32[]{:S(2)}) collective-permute-start(f32[4,3,8,256]{3,2,1,0:T(8,128)S(1)} %get-tuple-element.55), channel_id=1, source_target_pairs={{0,64},{64,128},{128,192},{1,65},{65,129},{129,193},{2,66},{66,130... | collective-permute-start | bytes 294920 | tf_op jit(solution)/shard_map/ppermute | solution.py:697
